TPU v7x, 32 devices: a whole 2x2x4 slice. The times are simulated.
32 devices in a mesh: group: 2 (over x), dp: 16 (over z, y, core).
Axes of the slice: x: 2, y: 2, z: 4, core: 2. Of those that a mesh axis runs over, the one named last changes fastest.
Arguments:
- activations: bfloat16 [128, 16, 16, 128], P(('group', 'dp')), parts along dimension 0, may hold values from -6 to 6
- cotangent: bfloat16 [64, 8, 8, 256], P(('group', 'dp')), parts along dimension 0, may hold values from -0.796875 to 0.796875
- shallow_weight: bfloat16 [3456, 128], P('dp'), may hold values from -0.109375 to 0.109375
- shallow_gain: bfloat16 [1, 128], P(None, 'dp'), may hold values from 0.099609375 to 1.8984375
- deep_weight: bfloat16 [3456, 256], P('dp'), may hold values from -0.109375 to 0.109375
- deep_gain: bfloat16 [1, 256], P(None, 'dp'), may hold values from 0.099609375 to 1.8984375
Outputs:
- input_grad: bfloat16 [128, 16, 16, 128], P(('group', 'dp')), parts along dimension 0
- shallow_weight_grad: float32 [6912, 128], P(('group', 'dp')), parts along dimension 0
- shallow_gain_grad: float32 [2, 128], P('group', 'dp'), parts along dimension 0
- deep_weight_grad: float32 [6912, 256], P(('group', 'dp')), parts along dimension 0
- deep_gain_grad: float32 [2, 256], P('group', 'dp'), parts along dimension 0
There are 2 independent parts, one for each index of `group`. A program takes and returns all parts, laid end to end along the dimension named above; an argument that names none is the same for every part. Nothing has to cross between parts.
All inputs are finite; a program needn't handle non-finite values.
Results may differ from a plain program's by a relative error of at most 0.017.
Values may be sent and summed in bfloat16 or wider, within the bound.
A program may use at most 64 MiB of HBM per device.

v0:
```python
import jax
import jax.numpy as jnp
from jax import lax
from jax.sharding import PartitionSpec as P


def gather_taps(padded, depth_tap, height_tap, cells_shape):
    cells_depth, cells_height, cells_width = cells_shape
    pieces = [
        padded[
            depth_tap : depth_tap + cells_depth,
            height_tap : height_tap + cells_height,
            width_tap : width_tap + cells_width,
        ]
        for width_tap in range(3)
    ]
    stacked = jnp.concatenate(pieces, axis=3)
    return stacked.reshape(cells_depth * cells_height * cells_width, -1)


def convolve(inputs, weight):
    cells_shape = inputs.shape[:3]
    channels = inputs.shape[3]
    padded = jnp.pad(inputs, ((1, 1), (1, 1), (1, 1), (0, 0)))
    summed = jnp.zeros(
        (cells_shape[0] * cells_shape[1] * cells_shape[2], weight.shape[1]), jnp.float32
    )
    for depth_tap in range(3):
        for height_tap in range(3):
            stacked = gather_taps(padded, depth_tap, height_tap, cells_shape)
            offset = (depth_tap * 3 + height_tap) * 3 * channels
            summed = summed + jnp.dot(
                stacked, weight[offset : offset + 3 * channels], preferred_element_type=jnp.float32
            )
    return summed.reshape(cells_shape[0], cells_shape[1], cells_shape[2], weight.shape[1])


def weight_grad(inputs, grad_out):
    cells_shape = inputs.shape[:3]
    padded = jnp.pad(inputs, ((1, 1), (1, 1), (1, 1), (0, 0)))
    grad_flat = grad_out.reshape(-1, grad_out.shape[3])
    blocks_list = []
    for depth_tap in range(3):
        for height_tap in range(3):
            stacked = gather_taps(padded, depth_tap, height_tap, cells_shape)
            blocks_list.append(
                lax.dot_general(
                    stacked, grad_flat, (((0,), (0,)), ((), ())), preferred_element_type=jnp.float32
                )
            )
    return jnp.concatenate(blocks_list, axis=0)


def input_grad_of(grad_out, weight):
    cells_depth, cells_height, cells_width = grad_out.shape[:3]
    channels = weight.shape[0] // 27
    grad_flat = grad_out.reshape(-1, grad_out.shape[3])
    accum = jnp.zeros((cells_depth + 2, cells_height + 2, cells_width + 2, channels), jnp.float32)
    for depth_tap in range(3):
        for height_tap in range(3):
            offset = (depth_tap * 3 + height_tap) * 3 * channels
            product = lax.dot_general(
                grad_flat,
                weight[offset : offset + 3 * channels],
                (((1,), (1,)), ((), ())),
                preferred_element_type=jnp.float32,
            )
            product = product.reshape(cells_depth, cells_height, cells_width, 3, channels)
            for width_tap in range(3):
                accum = accum.at[
                    depth_tap : depth_tap + cells_depth,
                    height_tap : height_tap + cells_height,
                    width_tap : width_tap + cells_width,
                ].add(product[:, :, :, width_tap])
    return accum[1:-1, 1:-1, 1:-1]


def norm_act(hidden, gain_row):
    center = hidden - jnp.mean(hidden, axis=(0, 1, 2), keepdims=True)
    spread = jnp.mean(center * center, axis=(0, 1, 2), keepdims=True)
    return jax.nn.silu(center * lax.rsqrt(spread + 1e-05) * gain_row[0])


def pool_act(hidden, gain_row):
    active = norm_act(hidden, gain_row)
    cells_depth, cells_height, cells_width, channels = active.shape
    blocks = active.reshape(
        cells_depth // 2, 2, cells_height // 2, 2, cells_width // 2, 2, channels
    )
    return jnp.mean(blocks, axis=(1, 3, 5))


def on_device(activations, cotangent, shallow_weight, shallow_gain, deep_weight, deep_gain):
    shallow_full, shallow_gfull = (
        lax.all_gather(shallow_weight, "dp", axis=0, tiled=True),
        lax.all_gather(shallow_gain, "dp", axis=1, tiled=True),
    )
    hidden_one = convolve(activations, shallow_full)
    pooled_float, back_one = jax.vjp(pool_act, hidden_one, shallow_gfull.astype(jnp.float32))
    pooled = pooled_float.astype(jnp.bfloat16)
    deep_full, deep_gfull = (
        lax.all_gather(deep_weight, "dp", axis=0, tiled=True),
        lax.all_gather(deep_gain, "dp", axis=1, tiled=True),
    )
    hidden_two = convolve(pooled, deep_full)
    output_two, back_two = jax.vjp(norm_act, hidden_two, deep_gfull.astype(jnp.float32))
    grad_hidden_two, grad_dgain = back_two(cotangent.astype(jnp.float32))
    grad_two = grad_hidden_two.astype(jnp.bfloat16)
    grad_deep = weight_grad(pooled, grad_two)
    grad_pooled = input_grad_of(grad_two, deep_full).astype(jnp.bfloat16)
    grad_hidden_one, grad_sgain = back_one(grad_pooled.astype(jnp.float32))
    grad_one = grad_hidden_one.astype(jnp.bfloat16)
    grad_shallow = weight_grad(activations, grad_one)
    grad_inputs = input_grad_of(grad_one, shallow_full).astype(jnp.bfloat16)
    shallow_share, sgain_share, deep_share, dgain_share = (
        lax.psum_scatter(grad_shallow, "dp", scatter_dimension=0, tiled=True),
        lax.psum_scatter(grad_sgain, "dp", scatter_dimension=1, tiled=True),
        lax.psum_scatter(grad_deep, "dp", scatter_dimension=0, tiled=True),
        lax.psum_scatter(grad_dgain, "dp", scatter_dimension=1, tiled=True),
    )
    return (grad_inputs, shallow_share, sgain_share, deep_share, dgain_share)


def solution(mesh):
    in_specs = (
        P(("group", "dp"), None, None, None),
        P(("group", "dp"), None, None, None),
        P("dp", None),
        P(None, "dp"),
        P("dp", None),
        P(None, "dp"),
    )
    out_specs = (
        P(("group", "dp"), None, None, None),
        P(("group", "dp"), None),
        P("group", "dp"),
        P(("group", "dp"), None),
        P("group", "dp"),
    )
    return jax.shard_map(
        on_device, mesh=mesh, in_specs=in_specs, out_specs=out_specs, check_vma=False
    )
```

profile of v0, /device:TPU:0, one launch (start us, length us, event | category | flops | bytes accessed | tf_op | source)
XLA Modules:
  0.0 333.0 jit_solution(13137294742068279423)
XLA Ops:
  8.0 5.8 %pad_slice_fusion.2 = (bf16[4,16,16,128]{3,2,1,0:T(8,128)(2,1)S(1)}, bf16[4,16,16,128]{3,2,1,0:T(8,128)(2,1)S(1)}, bf16[4,16,16,128]{3,2,1,0:T(8,128)(2,1)}, bf1...) fusion(bf16[4,16,16,128]{3,2,1,0:T(8,128)(2,1)} %param.114), kind=kLoop, calls=%fused_computation.2 | loop fusion | bytes 5242880 | tf_op jit(solution)/shard_map/slice | solution.py:10
  15.2 26.0 %all_gather.12 = bf16[3456,128]{1,0:T(8,128)(2,1)S(1)} all-gather(bf16[216,128]{1,0:T(8,128)(2,1)S(1)} %copy-done.113), channel_id=1, replica_groups=mesh['group'=2,'dp'=16] {'dp'}, dimensions={0}, use_global_device_ids=true | all-gather | bytes 940032 | tf_op jit(solution)/shard_map/all_gather | solution.py:95
  43.6 30.0 %all-reduce.8 = (bf16[128]{0:T(256)(128)(2,1)S(1)}, bf16[256]{0:T(256)(128)(2,1)S(1)}) all-reduce(bf16[128]{0:T(256)(128)(2,1)S(1)} %dynamic-update-slice.162, bf16[256]{0:T(256)(128)(2,1)S(1)} %dynamic-update-slice.163), channel_id=1, replica_groups=mesh['group'=2,'dp'=16] {'dp'}, use_global_device_ids=true, to_apply=%add.4 | all-reduce | flops 384 | bytes 1536
  93.0 1.9 fusion.94
  94.9 2.0 scatter-add.189
  105.4 1.7 scatter-add.226
  108.2 1.7 scatter-add.229
  112.3 1.9 scatter-add.231
  114.2 3.0 fusion.54
  117.3 3.6 %scatter-add.234 = f32[6,18,18,128]{3,2,1,0:T(8,128)S(1)} dynamic-update-slice(f32[6,18,18,128]{3,2,1,0:T(8,128)S(1)} %scatter-add.231, f32[4,16,16,128]{3,2,1,0:T(8,128)S(1)} %fusion.54, s32[]{:T(128)} %bitcast.37, s32[]{:T(128)} %bitcast.38, s32[]{:T(128)} %bitcast.39, s32[]{:T(128)} %constant.1475.clone.1) | dynamic-update-slice | bytes 1048580 | tf_op jit(solution)/shard_map/scatter-add | solution.py:74
  123.3 1.7 scatter-add.236
  125.1 2.5 fusion.150
  140.1 1.7 scatter-add.239
  144.1 1.9 scatter-add.241
  147.2 1.7 scatter-add.244
  160.9 1.7 scatter-add.246
  163.8 1.7 scatter-add.249
  167.1 1.7 scatter-add.251
  170.0 1.7 scatter-add.254
  176.2 1.7 scatter-add.259
  188.5 1.7 scatter-add.269
  191.0 29.5 %all-reduce.7 = f32[1,128]{1,0:T(1,128)S(1)} all-reduce(f32[1,128]{1,0:T(1,128)S(1)} %bitcast.638), channel_id=3, replica_groups=mesh['group'=2,'dp'=16] {'dp'}, use_global_device_ids=true, to_apply=%region_11.12.clone | all-reduce | flops 128 | bytes 1024
  222.3 32.9 %reduce-scatter.13.cloned.1.call-done = f32[216,128]{1,0:T(8,128)} async-done(((f32[3456,128]{1,0:T(8,128)}), f32[216,128]{1,0:T(8,128)}) %reduce-scatter.13.cloned.1.call-update) | async-done | bytes 110608
  255.2 71.3 %reduce-scatter.9.cloned.1.call-done = f32[216,256]{1,0:T(8,128)} async-done(((f32[3456,256]{1,0:T(8,128)}), f32[216,256]{1,0:T(8,128)}) %reduce-scatter.9.cloned.1.call-update) | async-done | bytes 221200 | tf_op jit(solution)/shard_map/reduce_scatter | solution.py:118
  (453 shorter events, 83.9 us)
Async XLA Ops:
  7.2 78.2 %all-gather.2.cloned.1.call-start = ((), (), s32[]{:S(2)}) async-start(), calls=%async_computation.3 | async-start | bytes 1880064 | tf_op jit(solution)/shard_map/all_gather | solution.py:102
  7.9 5.9 %copy-start.9 = (bf16[4,16,16,128]{3,2,1,0:T(8,128)(2,1)S(1)}, bf16[4,16,16,128]{3,2,1,0:T(8,128)(2,1)}, u32[]{:S(2)}) copy-start(bf16[4,16,16,128]{3,2,1,0:T(8,128)(2,1)} %param.114) | copy-start | bytes 786436
  7.9 213.1 %reduce-scatter.11.cloned.1.call-start = ((), (), s32[]{:S(2)}) async-start(), calls=%async_computation.5 | async-start | bytes 139264
  13.8 61.7 %copy-start.38 = (bf16[4,16,16,128]{3,2,1,0:T(8,128)(2,1)}, bf16[4,16,16,128]{3,2,1,0:T(8,128)(2,1)S(1)}, u32[]{:S(2)}) copy-start(bf16[4,16,16,128]{3,2,1,0:T(8,128)(2,1)S(1)} %get-tuple-element.682) | copy-start | bytes 786436
  13.8 61.7 %copy-start.40 = (bf16[4,16,16,128]{3,2,1,0:T(8,128)(2,1)}, bf16[4,16,16,128]{3,2,1,0:T(8,128)(2,1)S(1)}, u32[]{:S(2)}) copy-start(bf16[4,16,16,128]{3,2,1,0:T(8,128)(2,1)S(1)} %get-tuple-element.683) | copy-start | bytes 786436
  13.8 61.7 %copy-start.42 = (bf16[4,16,16,128]{3,2,1,0:T(8,128)(2,1)}, bf16[4,16,16,128]{3,2,1,0:T(8,128)(2,1)S(1)}, u32[]{:S(2)}) copy-start(bf16[4,16,16,128]{3,2,1,0:T(8,128)(2,1)S(1)} %get-tuple-element.684) | copy-start | bytes 786436
  13.8 61.7 %copy-start.44 = (bf16[4,16,16,128]{3,2,1,0:T(8,128)(2,1)}, bf16[4,16,16,128]{3,2,1,0:T(8,128)(2,1)S(1)}, u32[]{:S(2)}) copy-start(bf16[4,16,16,128]{3,2,1,0:T(8,128)(2,1)S(1)} %get-tuple-element.680) | copy-start | bytes 786436
  13.8 64.1 %copy-start.16 = (bf16[4,16,16,128]{3,2,1,0:T(8,128)(2,1)}, bf16[4,16,16,128]{3,2,1,0:T(8,128)(2,1)S(1)}, u32[]{:S(2)}) copy-start(bf16[4,16,16,128]{3,2,1,0:T(8,128)(2,1)S(1)} %get-tuple-element.693) | copy-start | bytes 786436
  13.8 67.5 %copy-start.10 = (bf16[4,16,16,128]{3,2,1,0:T(8,128)(2,1)}, bf16[4,16,16,128]{3,2,1,0:T(8,128)(2,1)S(1)}, u32[]{:S(2)}) copy-start(bf16[4,16,16,128]{3,2,1,0:T(8,128)(2,1)S(1)} %get-tuple-element.679) | copy-start | bytes 786436
  13.8 67.5 %copy-start.12 = (bf16[4,16,16,128]{3,2,1,0:T(8,128)(2,1)}, bf16[4,16,16,128]{3,2,1,0:T(8,128)(2,1)S(1)}, u32[]{:S(2)}) copy-start(bf16[4,16,16,128]{3,2,1,0:T(8,128)(2,1)S(1)} %get-tuple-element.696) | copy-start | bytes 786436
  13.8 67.5 %copy-start.14 = (bf16[4,16,16,128]{3,2,1,0:T(8,128)(2,1)}, bf16[4,16,16,128]{3,2,1,0:T(8,128)(2,1)S(1)}, u32[]{:S(2)}) copy-start(bf16[4,16,16,128]{3,2,1,0:T(8,128)(2,1)S(1)} %get-tuple-element.697) | copy-start | bytes 786436
  13.9 27.3 %copy-start.125 = (u32[32]{0:T(128)S(1)}, u32[32]{0:T(128)}, u32[]{:S(2)}) copy-start(u32[32]{0:T(128)} %constant.1493) | copy-start | bytes 388
  13.9 29.2 %copy-start.129 = (bf16[1,8]{1,0:T(2,128)(2,1)S(1)}, bf16[1,8]{1,0:T(2,128)(2,1)}, u32[]{:S(2)}) copy-start(bf16[1,8]{1,0:T(2,128)(2,1)} %param.117) | copy-start | bytes 52
  13.9 29.4 %copy-start.130 = (bf16[1,16]{1,0:T(2,128)(2,1)S(1)}, bf16[1,16]{1,0:T(2,128)(2,1)}, u32[]{:S(2)}) copy-start(bf16[1,16]{1,0:T(2,128)(2,1)} %param.119) | copy-start | bytes 100
  73.6 28.7 %copy-start.116 = (f32[128]{0:T(128)}, f32[128]{0:T(128)S(1)}, u32[]{:S(2)}) copy-start(f32[128]{0:T(128)S(1)} %mul.291) | copy-start | bytes 1540
  82.8 19.6 %copy-start.114 = (f32[128]{0:T(128)}, f32[128]{0:T(128)S(1)}, u32[]{:S(2)}) copy-start(f32[128]{0:T(128)S(1)} %broadcast_multiply_fusion.1) | copy-start | bytes 1540
  82.9 19.4 %copy-start.118 = (f32[128]{0:T(128)}, f32[128]{0:T(128)S(1)}, u32[]{:S(2)}) copy-start(f32[128]{0:T(128)S(1)} %fusion.119) | copy-start | bytes 1540
  85.4 4.6 %copy-start = (bf16[3456,256]{1,0:T(8,128)(2,1)S(1)}, bf16[3456,256]{1,0:T(8,128)(2,1)}, u32[]{:S(2)}) copy-start(bf16[3456,256]{1,0:T(8,128)(2,1)} %all-gather.2.cloned.1.call-done) | copy-start | bytes 5308420
  125.1 3.0 copy-start.45
  125.1 3.0 copy-start.46
  125.1 3.0 copy-start.53
  138.9 116.2 %reduce-scatter.13.cloned.1.call-start = ((), (), s32[]{:S(2)}) async-start(), calls=%async_computation.6 | async-start | bytes 1880064
  141.8 184.7 %reduce-scatter.9.cloned.1.call-start = ((), (), s32[]{:S(2)}) async-start(), calls=%async_computation.4 | async-start | bytes 3760128 | tf_op jit(solution)/shard_map/reduce_scatter | solution.py:118
  187.4 3.6 %copy-start.126 = (f32[128]{0:T(128)S(1)}, f32[128]{0:T(128)}, u32[]{:S(2)}) copy-start(f32[128]{0:T(128)} %get-tuple-element.653) | copy-start | bytes 1540
  (111 other events, 147.4 us)
Sparse Core Ops, SparseCore 0:
  10.2 45.6 all-gather.1
  139.1 52.4 reduce-scatter.10
  195.9 59.2 reduce-scatter.12
  259.5 66.9 reduce-scatter.8
where the time goes:
time: 334 us; the launch traced here: 333 us
  waiting for transfers between devices  105 us (31%)
  blocking collectives  85.5 us (26%)
  local copies, waits for them, and re-layouts  62.3 us (19%)
  matrix products  37 us (11%)
  other arithmetic  24.9 us (7%)
  between operations  18.2 us (5%)
    reduce_scatter x1, waiting for transfers between devices, on_device(): lax.psum_scatter(grad_deep, 'dp', scatter_dimension=0, tiled=True)  71.3 us
    unnamed x2, blocking collectives  59.5 us
    scatter-add x38, local copies, waits for them, and re-layouts, input_grad_of(): accum = accum.at[depth_tap:depth_tap + cells_depth, height_tap:height_tap...  37.4 us
    unnamed x6, waiting for transfers between devices  33.6 us
    all_gather x1, blocking collectives, on_device(): lax.all_gather(shallow_weight, 'dp', axis=0, tiled=True)  26 us
    dot_general x18, matrix products, weight_grad(): lax.dot_general(stacked, grad_flat, (((0,), (0,)), ((), ())), preferred_e...  19 us
    add x36, other arithmetic, input_grad_of(): accum = accum.at[depth_tap:depth_tap + cells_depth, height_tap:height_tap...  15.9 us
    unnamed x270, local copies, waits for them, and re-layouts  15.1 us
  transfers between devices with their start and end apart: 4, of which 2 were waited for; matrix products, arithmetic and copies ran while one was open for 19% of the time, Pallas kernels for 0%

commit v1 on v0

v1 whole, which is shorter than its diff:
```python
import functools

import jax
import jax.numpy as jnp
from jax import lax
from jax.experimental import pallas as pl
from jax.experimental.pallas import tpu as pltpu
from jax.sharding import PartitionSpec as P

MESH = pl.DeviceIdType.MESH
LANES = 128
CONV_DIMS = ("NDHWC", "DHWIO", "NDHWC")
GRAD_DIMS = ("CDHWN", "IDHWO", "DHWNC")


def convolve(inputs, weight):
    kernel = weight.reshape(3, 3, 3, inputs.shape[3], -1)
    return lax.conv_general_dilated(
        inputs[None],
        kernel,
        (1, 1, 1),
        ((1, 1),) * 3,
        dimension_numbers=CONV_DIMS,
        preferred_element_type=jnp.float32,
    )[0]


def weight_grad(inputs, grad_out):
    grad = lax.conv_general_dilated(
        inputs[None],
        grad_out[None],
        (1, 1, 1),
        ((1, 1),) * 3,
        dimension_numbers=GRAD_DIMS,
        preferred_element_type=jnp.float32,
    )
    return grad.reshape(27 * inputs.shape[3], -1)


def transposed(weight):
    channels = weight.shape[0] // 27
    flipped = weight.reshape(27, channels, -1)[::-1]
    return flipped.transpose(0, 2, 1).reshape(-1, channels)


def norm_act(hidden, gain_row):
    center = hidden - jnp.mean(hidden, axis=(0, 1, 2), keepdims=True)
    spread = jnp.mean(center * center, axis=(0, 1, 2), keepdims=True)
    return jax.nn.silu(center * lax.rsqrt(spread + 1e-05) * gain_row[0])


def pool_act(hidden, gain_row):
    active = norm_act(hidden, gain_row)
    cells_depth, cells_height, cells_width, channels = active.shape
    blocks = active.reshape(
        cells_depth // 2, 2, cells_height // 2, 2, cells_width // 2, 2, channels
    )
    return jnp.mean(blocks, axis=(1, 3, 5))


def partners(me, steps):
    bits = [lax.rem(me // 2**step, 2) for step in range(steps)]
    peers = [me + 2**step - 2 ** (step + 1) * bits[step] for step in range(steps)]
    return bits, peers


def greet(peers):
    barrier = pltpu.get_barrier_semaphore()
    for peer in peers:
        pl.semaphore_signal(barrier, inc=1, device_id={"dp": peer}, device_id_type=MESH)
    pl.semaphore_wait(barrier, len(peers))


def gather_kernel(steps, pieces, x_ref, out_ref, send_sem, recv_sem):
    count = 2**steps
    bits, peers = partners(lax.axis_index("dp"), steps)
    starts = [
        sum(bits[low] * (count >> (low + 1)) for low in range(step + 1)) for step in range(steps)
    ]
    for piece in range(pieces):
        out_ref[piece, starts[-1]] = x_ref[piece]
    greet(peers)
    copies = {}
    for wave in range(steps + pieces):
        for piece in range(pieces):
            turn = wave - piece
            if turn >= 1 and turn <= steps:
                copies[piece, turn - 1].wait_recv()
            if turn >= 0 and turn < steps:
                step = steps - 1 - turn
                held = out_ref.at[piece, pl.ds(starts[step], count >> (step + 1))]
                copies[piece, turn] = pltpu.make_async_remote_copy(
                    src_ref=held,
                    dst_ref=held,
                    send_sem=send_sem.at[piece, turn],
                    recv_sem=recv_sem.at[piece, turn],
                    device_id={"dp": peers[step]},
                    device_id_type=MESH,
                )
                copies[piece, turn].start()
    for copy in copies.values():
        copy.wait_send()


def reduce_kernel(steps, pieces, x_ref, out_ref, work_ref, recv_ref, send_sem, recv_sem):
    count = 2**steps
    bits, peers = partners(lax.axis_index("dp"), steps)
    greet(peers)
    copies = {}

    def send(piece, step, source):
        size = count >> (step + 1)
        copies[piece, step] = pltpu.make_async_remote_copy(
            src_ref=source,
            dst_ref=recv_ref.at[piece, pl.ds(size, size)],
            send_sem=send_sem.at[piece, step],
            recv_sem=recv_sem.at[piece, step],
            device_id={"dp": peers[step]},
            device_id_type=MESH,
        )
        copies[piece, step].start()

    def total(piece, step, place):
        size = count >> (step + 1)
        if step == 0:
            mine = x_ref[piece, bits[0] * size + place]
        else:
            mine = work_ref[piece, 2 * size + bits[step] * size + place]
        theirs = recv_ref[piece, size + place]
        return mine.astype(jnp.float32) + theirs.astype(jnp.float32)

    def add_range(piece, step, first, length):
        size = count >> (step + 1)

        def body(index, carry):
            place = first + index
            work_ref[piece, size + place] = total(piece, step, place).astype(jnp.bfloat16)
            return carry

        lax.fori_loop(0, length, body, 0)

    for piece in range(pieces):
        half = count // 2
        send(piece, 0, x_ref.at[piece, pl.ds((1 - bits[0]) * half, half)])
    for wave in range(steps + pieces - 1):
        for piece in range(pieces):
            step = wave - piece
            if step < 0 or step >= steps:
                continue
            copies[piece, step].wait_recv()
            if step == steps - 1:
                out_ref[piece] = total(piece, step, 0)
                continue
            size = count >> (step + 1)
            part = size // 2
            away = (1 - bits[step + 1]) * part
            add_range(piece, step, away, part)
            send(piece, step + 1, work_ref.at[piece, pl.ds(size + away, part)])
            add_range(piece, step, bits[step + 1] * part, part)
    for copy in copies.values():
        copy.wait_send()


def bit_reversed(array, steps):
    split = array.reshape((array.shape[0],) + (2,) * steps + array.shape[2:])
    tail = tuple(range(steps + 1, split.ndim))
    turned = split.transpose((0,) + tuple(range(steps, 0, -1)) + tail)
    return turned.reshape(array.shape)


def gather(packed, count):
    pieces, rows, lanes = packed.shape
    steps = count.bit_length() - 1
    full = pl.pallas_call(
        functools.partial(gather_kernel, steps, pieces),
        out_shape=jax.ShapeDtypeStruct((pieces, count, rows, lanes), packed.dtype),
        in_specs=[pl.BlockSpec(memory_space=pltpu.VMEM)],
        out_specs=pl.BlockSpec(memory_space=pltpu.VMEM),
        scratch_shapes=[pltpu.SemaphoreType.DMA((pieces, steps))] * 2,
        compiler_params=pltpu.CompilerParams(
            collective_id=0, has_side_effects=True, vmem_limit_bytes=24 << 20
        ),
    )(packed)
    return bit_reversed(full, steps)


def reduce_scatter(packed, count):
    pieces, _, rows, lanes = packed.shape
    steps = count.bit_length() - 1
    return pl.pallas_call(
        functools.partial(reduce_kernel, steps, pieces),
        out_shape=jax.ShapeDtypeStruct((pieces, rows, lanes), jnp.float32),
        in_specs=[pl.BlockSpec(memory_space=pltpu.VMEM)],
        out_specs=pl.BlockSpec(memory_space=pltpu.VMEM),
        scratch_shapes=[
            pltpu.VMEM(packed.shape, jnp.bfloat16),
            pltpu.VMEM(packed.shape, jnp.bfloat16),
            pltpu.SemaphoreType.DMA((pieces, steps)),
            pltpu.SemaphoreType.DMA((pieces, steps)),
        ],
        compiler_params=pltpu.CompilerParams(
            collective_id=1, has_side_effects=True, vmem_limit_bytes=40 << 20
        ),
    )(bit_reversed(packed, steps))


def pack(blocks, gains):
    pieces = []
    for block, gain in zip(blocks, gains):
        _, rows, channels = block.shape
        below = -(-(rows + 1) // 16) * 16 - rows
        gain_rows = jnp.pad(
            gain[:, None, :], ((0, 0), (0, below - 1), (0, LANES - gain.shape[1]))
        )
        for lane in range(0, channels, LANES):
            pieces.append(
                jnp.concatenate([block[:, :, lane : lane + LANES], gain_rows], axis=1)
            )
    return jnp.stack(pieces)


def on_device(
    count, activations, cotangent, shallow_weight, shallow_gain, deep_weight, deep_gain
):
    rows, shallow_width = shallow_weight.shape
    deep_width = deep_weight.shape[1]
    shallow_pieces = shallow_width // LANES
    shallow_part, deep_part = shallow_gain.shape[1], deep_gain.shape[1]
    full = gather(
        pack((shallow_weight[None], deep_weight[None]), (shallow_gain, deep_gain))[:, 0], count
    )

    def unpack(first, width):
        lanes = [full[first + index, :, :rows] for index in range(width // LANES)]
        return jnp.concatenate(lanes, axis=2).reshape(count * rows, width)

    shallow_full = unpack(0, shallow_width)
    deep_full = unpack(shallow_pieces, deep_width)
    shallow_gfull = full[0, :, rows, :shallow_part].reshape(1, -1).astype(jnp.float32)
    deep_gfull = full[shallow_pieces, :, rows, :deep_part].reshape(1, -1).astype(jnp.float32)

    hidden_one = convolve(activations, shallow_full)
    pooled_float, back_one = jax.vjp(pool_act, hidden_one, shallow_gfull)
    pooled = pooled_float.astype(jnp.bfloat16)
    hidden_two = convolve(pooled, deep_full)
    _, back_two = jax.vjp(norm_act, hidden_two, deep_gfull)
    grad_hidden_two, grad_dgain = back_two(cotangent.astype(jnp.float32))
    grad_two = grad_hidden_two.astype(jnp.bfloat16)
    grad_deep = weight_grad(pooled, grad_two)
    grad_pooled = convolve(grad_two, transposed(deep_full)).astype(jnp.bfloat16)
    grad_hidden_one, grad_sgain = back_one(grad_pooled.astype(jnp.float32))
    grad_one = grad_hidden_one.astype(jnp.bfloat16)
    grad_shallow = weight_grad(activations, grad_one)
    grad_inputs = convolve(grad_one, transposed(shallow_full)).astype(jnp.bfloat16)

    packed = pack(
        (
            grad_shallow.astype(jnp.bfloat16).reshape(count, rows, -1),
            grad_deep.astype(jnp.bfloat16).reshape(count, rows, -1),
        ),
        (
            grad_sgain.astype(jnp.bfloat16).reshape(count, -1),
            grad_dgain.astype(jnp.bfloat16).reshape(count, -1),
        ),
    )
    shares = reduce_scatter(packed, count)
    shallow_share = jnp.concatenate(
        [shares[index, :rows] for index in range(shallow_pieces)], axis=1
    )
    deep_share = jnp.concatenate(
        [shares[index, :rows] for index in range(shallow_pieces, shares.shape[0])], axis=1
    )
    sgain_share = shares[0, rows : rows + 1, :shallow_part]
    dgain_share = shares[shallow_pieces, rows : rows + 1, :deep_part]
    return (grad_inputs, shallow_share, sgain_share, deep_share, dgain_share)


def solution(mesh):
    in_specs = (
        P(("group", "dp"), None, None, None),
        P(("group", "dp"), None, None, None),
        P("dp", None),
        P(None, "dp"),
        P("dp", None),
        P(None, "dp"),
    )
    out_specs = (
        P(("group", "dp"), None, None, None),
        P(("group", "dp"), None),
        P("group", "dp"),
        P(("group", "dp"), None),
        P("group", "dp"),
    )
    return jax.shard_map(
        functools.partial(on_device, mesh.shape["dp"]),
        mesh=mesh,
        in_specs=in_specs,
        out_specs=out_specs,
        check_vma=False,
    )
```

time: 334 us -> 105 us (0.31)
  waiting for transfers between devices: 105 us -> 0 us
  blocking collectives: 85.5 us -> 0 us
  Pallas kernels: 0 us -> 63.6 us
  local copies, waits for them, and re-layouts: 62.3 us -> 11.6 us
  other arithmetic: 24.9 us -> 4.86 us
  between operations: 18.2 us -> 0.96 us
  matrix products: 37 us -> 23.2 us
    reduce_scatter x1 -> x0, waiting for transfers between devices: 71.3 us -> none  [on_device(): lax.psum_scatter(grad_deep, 'dp', scatter_dimension=0, tiled=True)]
    pallas_call x0 -> x2, Pallas kernels: none -> 63.6 us  [the longest x1 32.6 us: gather(): pl.pallas_call(functools.partial(gather_kernel, steps, pieces), out_shape...]
    unnamed x2 -> x0, blocking collectives: 59.5 us -> none
    scatter-add x38 -> x0, local copies, waits for them, and re-layouts: 37.4 us -> none  [input_grad_of(): accum = accum.at[depth_tap:depth_tap + cells_depth, height_tap:height_tap...]
    dot_general x54 -> x0, matrix products: 37 us -> none  [the longest x18 19 us: weight_grad(): lax.dot_general(stacked, grad_flat, (((0,), (0,)), ((), ())), preferred_e...]
    unnamed x6 -> x0, waiting for transfers between devices: 33.6 us -> none
    all_gather x1 -> x0, blocking collectives: 26 us -> none  [on_device(): lax.all_gather(shallow_weight, 'dp', axis=0, tiled=True)]
    conv_general_dilated x0 -> x6, matrix products: none -> 23.2 us  [the longest x4 14.7 us: convolve(): lax.conv_general_dilated(inputs[None], kernel, (1, 1, 1), ((1, 1),) * 3,...]
  transfers between devices with their start and end apart: 4 -> 0, of which waited for: 2 -> 0; matrix products, arithmetic and copies ran while one was open for 19% -> 0% of each run, Pallas kernels for 0% -> 0%
where the time goes in v1:
time: 105 us; the launch traced here: 104 us
  Pallas kernels  63.6 us (61%)
  matrix products  23.2 us (22%)
  local copies, waits for them, and re-layouts  11.6 us (11%)
  other arithmetic  4.86 us (5%)
    pallas_call x1, Pallas kernels, gather(): pl.pallas_call(functools.partial(gather_kernel, steps, pieces), out_shape...  32.6 us
    pallas_call x1, Pallas kernels, reduce_scatter(): pl.pallas_call(functools.partial(reduce_kernel, steps, pieces), out_shape...  31.1 us
    conv_general_dilated x4, matrix products, convolve(): lax.conv_general_dilated(inputs[None], kernel, (1, 1, 1), ((1, 1),) * 3,...  14.7 us
    conv_general_dilated x2, matrix products, weight_grad(): lax.conv_general_dilated(inputs[None], grad_out[None], (1, 1, 1), ((1, 1)...  8.52 us
    unnamed x22, local copies, waits for them, and re-layouts  3.44 us
    rev x2, local copies, waits for them, and re-layouts, transposed(): flipped = weight.reshape(27, channels, -1)[::-1]  2.33 us

profile of v1, /device:TPU:0, one launch (start us, length us, event | category | flops | bytes accessed | tf_op | source)
XLA Modules:
  0.0 104.2 jit_solution(12437889413117021199)
XLA Ops:
  0.6 0.9 fusion.60
  1.5 0.9 fusion.44
  2.4 32.6 %shard_map.101 = bf16[3,16,224,128]{3,2,1,0:T(8,128)(2,1)S(1)} custom-call(bf16[3,224,128]{2,1,0:T(8,128)(2,1)S(1)} %maximum_bitcast_fusion.1.x_ref), custom_call_target="tpu_custom_call" | custom-call | tf_op jit(solution)/shard_map/pallas_call | solution.py:174
  35.4 1.5 %fusion.58 = (bf16[1,16,216,128]{3,2,1,0:T(8,128)(2,1)}, bf16[1,16,216,128]{3,2,1,0:T(8,128)(2,1)}, bf16[1,16,216,128]{3,2,1,0:T(8,128)(2,1)}) fusion(bf16[3,16,224,128]{3,2,1,0:T(8,128)(2,1)S(1)} %bitcast.99), kind=kLoop, calls=%fused_computation.103 | loop fusion | bytes 5308416 | tf_op jit(solution)/shard_map/slice | solution.py:234
  37.1 7.1 %fusion.61 = (f32[128]{0:T(128)S(1)}, f32[1,4,16,16,128]{4,0,3,2,1:T(1,128)S(1)}) fusion(bf16[3,3,3,128,128]{4,3,2,1,0:T(8,128)(2,1)} %bitcast.114, bf16[1,4,16,16,128]{4,3,2,1,0:T(8,128)(2,1)S(1)} %bitcast.126), kind=kOutput, calls=%fused_computation.106 | convolution fusion | flops 693501824 | bytes 1671680 | tf_op jit(solution)/shard_map/conv_general_dilated | solution.py:18
  44.6 1.3 %fusion.62 = (f32[256]{0:T(256)S(1)}, f32[1,2,8,8,256]{4,0,3,2,1:T(1,128)S(1)}) fusion(bf16[3,3,3,128,128]{4,3,2,1,0:T(8,128)(2,1)S(1)} %bitcast.112, bf16[3,3,3,128,128]{4,3,2,1,0:T(8,128)(2,1)S(1)} %bitcast.110, bf16[1,2,8,8,128]{4,3,2,1,0:T(8,128)(2,1)S(1)} %fusion.47), kind=kOutput, calls=%fused_computation.107 | convolution fusion | flops 130449152 | bytes 1934336 | tf_op jit(solution)/shard_map/conv_general_dilated | solution.py:18
  46.5 1.0 rev.7
  47.5 1.1 %convolution_convert_fusion = bf16[3,3,3,128,256]{4,3,2,1,0:T(8,128)(2,1)S(1)} fusion(bf16[1,2,8,8,256]{4,3,2,1,0:T(8,128)(2,1)S(1)} %fusion.38, bf16[1,2,8,8,128]{4,3,2,1,0:T(8,128)(2,1)S(1)} %fusion.47), kind=kOutput, calls=%fused_computation.9 | convolution fusion | flops 127762432 | bytes 1867776 | tf_op jit(solution)/shard_map/conv_general_dilated | solution.py:29
  48.9 1.1 %fusion.11 = (bf16[16,224,128]{2,1,0:T(8,128)(2,1)S(1)}, bf16[16,224,128]{2,1,0:T(8,128)(2,1)}) fusion(bf16[16,1,16]{2,1,0:T(2,128)(2,1)S(1)} %convert_element_type.137, bf16[16,216,128]{2,1,0:T(8,128)(2,1)S(1)} %get-tuple-element.29, bf16[16,216,128]{2,1,0:T(8,128)(2,1)S(1)} %get-tuple-element.30), kind=kLoop, calls=%fused_computation.19 | loop fusion | flops 4128768 | bytes 3604992 | tf_op jit(solution)/shard_map/concatenate | solution.py:217
  50.2 0.4 copy-done.4
  50.9 1.3 %rev.6 = bf16[27,128,256]{2,1,0:T(8,128)(2,1)} reverse(bf16[27,128,256]{2,1,0:T(8,128)(2,1)S(1)} %pad_maximum_fusion), dimensions={0} | reverse | bytes 3538944 | tf_op jit(solution)/shard_map/rev | solution.py:42
  52.2 3.3 %fusion.9 = f32[1,2,8,8,128]{4,0,3,2,1:T(1,128)S(1)} fusion(bf16[3,3,3,256,128]{3,4,2,1,0:T(8,128)(2,1)} %bitcast.116, bf16[1,2,8,8,256]{4,3,2,1,0:T(8,128)(2,1)S(1)} %fusion.38), kind=kOutput, calls=%fused_computation.17 | convolution fusion | flops 126926848 | bytes 1900544 | tf_op jit(solution)/shard_map/conv_general_dilated | solution.py:18
  55.7 0.3 multiply_reduce_fusion
  56.1 0.3 fusion.57
  57.0 0.8 copy-done.6
  57.7 2.9 %fusion.7 = bf16[4,16,8,3,128]{4,2,3,1,0:T(8,128)(2,1)S(1)} fusion(bf16[3,3,3,128,128]{3,4,2,1,0:T(8,128)(2,1)S(1)} %bitcast.119, bf16[4,16,1,7,2,128]{5,3,4,1,0,2:T(8,128)(2,1)S(1)} %slice.65, bf16[4,16,1,8,3,128]{5,3,4,1,0,2:T(8,128)(2,1)S(1)} %copy.68, pred[8,3]{0,1:T(4,128)(4,1)S(1)} %copy-done.9), kind=kOutput, calls=%fused_computation.14 | convolution fusion | flops 1087635456 | bytes 1900568 | tf_op jit(solution)/shard_map/conv_general_dilated | solution.py:18
  60.8 0.8 copy.78
  61.5 7.4 %convolution_convert_fusion.1 = bf16[3,3,3,128,128]{4,3,2,1,0:T(8,128)(2,1)S(1)} fusion(bf16[1,4,16,16,128]{4,3,2,1,0:T(8,128)(2,1)S(1)} %add_convert_fusion, bf16[1,4,16,16,128]{4,3,2,1,0:T(8,128)(2,1)S(1)} %bitcast.127), kind=kOutput, calls=%fused_computation.10 | convolution fusion | flops 693813248 | bytes 1409024 | tf_op jit(solution)/shard_map/conv_general_dilated | solution.py:29
  69.1 1.1 %copy-done = bf16[16,224,128]{2,1,0:T(8,128)(2,1)S(1)} copy-done((bf16[16,224,128]{2,1,0:T(8,128)(2,1)S(1)}, bf16[16,224,128]{2,1,0:T(8,128)(2,1)}, u32[]{:S(2)}) %copy-start) | copy-done | bytes 917528
  70.8 31.1 %shard_map.102 = f32[3,224,128]{2,1,0:T(8,128)S(1)} custom-call(bf16[3,16,224,128]{3,2,1,0:T(8,128)(2,1)S(1)} %bitcast.96), custom_call_target="tpu_custom_call" | custom-call | tf_op jit(solution)/shard_map/pallas_call | solution.py:190
  101.9 0.5 slice_bitcast_fusion.5
  102.4 0.5 slice_bitcast_fusion.4
  102.9 0.7 slice_bitcast_fusion.2
  103.5 0.7 pad_maximum_fusion.1
  (54 shorter events, 3.7 us)
Async XLA Ops:
  35.4 1.6 %copy-start.8 = (bf16[4,16,16,128]{3,2,1,0:T(8,128)(2,1)S(1)}, bf16[4,16,16,128]{3,2,1,0:T(8,128)(2,1)}, u32[]{:S(2)}) copy-start(bf16[4,16,16,128]{3,2,1,0:T(8,128)(2,1)} %param.6) | copy-start | bytes 786436
  37.1 7.5 %copy-start.1 = (bf16[1,16,216,128]{3,2,1,0:T(8,128)(2,1)S(1)}, bf16[1,16,216,128]{3,2,1,0:T(8,128)(2,1)}, u32[]{:S(2)}) copy-start(bf16[1,16,216,128]{3,2,1,0:T(8,128)(2,1)} %get-tuple-element.26) | copy-start | bytes 2654212
  37.1 7.5 %copy-start.3 = (bf16[1,16,216,128]{3,2,1,0:T(8,128)(2,1)S(1)}, bf16[1,16,216,128]{3,2,1,0:T(8,128)(2,1)}, u32[]{:S(2)}) copy-start(bf16[1,16,216,128]{3,2,1,0:T(8,128)(2,1)} %get-tuple-element.27) | copy-start | bytes 2654212
  44.6 1.4 %copy-start.7 = (bf16[2,8,8,256]{3,2,1,0:T(8,128)(2,1)S(1)}, bf16[2,8,8,256]{3,2,1,0:T(8,128)(2,1)}, u32[]{:S(2)}) copy-start(bf16[2,8,8,256]{3,2,1,0:T(8,128)(2,1)} %param.7) | copy-start | bytes 196612
  44.6 1.9 %copy-start.5 = (bf16[1,16,216,128]{3,2,1,0:T(8,128)(2,1)S(1)}, bf16[1,16,216,128]{3,2,1,0:T(8,128)(2,1)}, u32[]{:S(2)}) copy-start(bf16[1,16,216,128]{3,2,1,0:T(8,128)(2,1)} %get-tuple-element.28) | copy-start | bytes 2654212
  48.9 1.4 %copy-start.2 = (bf16[1,16,216,128]{3,2,1,0:T(8,128)(2,1)S(1)}, bf16[1,16,216,128]{3,2,1,0:T(8,128)(2,1)}, u32[]{:S(2)}) copy-start(bf16[1,16,216,128]{3,2,1,0:T(8,128)(2,1)} %get-tuple-element.26) | copy-start | bytes 2654212
  48.9 1.8 %copy-start.4 = (bf16[1,16,216,128]{3,2,1,0:T(8,128)(2,1)S(1)}, bf16[1,16,216,128]{3,2,1,0:T(8,128)(2,1)}, u32[]{:S(2)}) copy-start(bf16[1,16,216,128]{3,2,1,0:T(8,128)(2,1)} %get-tuple-element.27) | copy-start | bytes 2654212
  56.6 1.2 %copy-start.6 = (bf16[27,128,128]{2,1,0:T(8,128)(2,1)S(1)}, bf16[27,128,128]{2,1,0:T(8,128)(2,1)}, u32[]{:S(2)}) copy-start(bf16[27,128,128]{2,1,0:T(8,128)(2,1)} %rev.7) | copy-start | bytes 2654212
  56.6 1.2 %copy-start.9 = (pred[8,3]{0,1:T(4,128)(4,1)S(1)}, pred[8,3]{0,1:T(4,128)(4,1)}, u32[]{:S(2)}) copy-start(pred[8,3]{0,1:T(4,128)(4,1)} %constant.49) | copy-start | bytes 76
  69.0 1.2 %copy-start = (bf16[16,224,128]{2,1,0:T(8,128)(2,1)S(1)}, bf16[16,224,128]{2,1,0:T(8,128)(2,1)}, u32[]{:S(2)}) copy-start(bf16[16,224,128]{2,1,0:T(8,128)(2,1)} %get-tuple-element.37) | copy-start | bytes 2752516

commit v2 on v1

--- a/solution.py
+++ b/solution.py
@@ -71,117 +71,126 @@
     pl.semaphore_wait(barrier, len(peers))
 
 
+def lowest(mask):
+    return (mask & -mask).bit_length() - 1
+
+
+def chunk_of(bits, mask):
+    return sum(
+        ((1 - bit) if mask >> step & 1 else bit) * 2**step for step, bit in enumerate(bits)
+    )
+
+
+def send_order(steps):
+    masks = [mask for mask in range(1, 2**steps) if lowest(mask) > 0]
+
+    def key(mask):
+        step = lowest(mask)
+        return 1 - (mask - 2**step) / 2**steps + 0.3 * (step - 1)
+
+    return sorted(masks, key=key)
+
+
 def gather_kernel(steps, pieces, x_ref, out_ref, send_sem, recv_sem):
-    count = 2**steps
     bits, peers = partners(lax.axis_index("dp"), steps)
-    starts = [
-        sum(bits[low] * (count >> (low + 1)) for low in range(step + 1)) for step in range(steps)
-    ]
+    mine = chunk_of(bits, 0)
     for piece in range(pieces):
-        out_ref[piece, starts[-1]] = x_ref[piece]
+        out_ref[piece, mine] = x_ref[piece]
     greet(peers)
-    copies = {}
-    for wave in range(steps + pieces):
+    sends = []
+
+    def copy_of(piece, mask, step):
+        held = out_ref.at[piece, chunk_of(bits, mask)]
+        there = mask | 1 << step
+        return pltpu.make_async_remote_copy(
+            src_ref=held,
+            dst_ref=held,
+            send_sem=send_sem.at[piece, there],
+            recv_sem=recv_sem.at[piece, there],
+            device_id={"dp": peers[step]},
+            device_id_type=MESH,
+        )
+
+    def send(piece, mask, step):
+        copy = copy_of(piece, mask, step)
+        copy.start()
+        sends.append(copy)
+
+    def arrive(piece, mask):
+        landed = out_ref.at[piece, chunk_of(bits, mask)]
+        pltpu.make_async_remote_copy(
+            src_ref=landed,
+            dst_ref=landed,
+            send_sem=send_sem.at[piece, mask],
+            recv_sem=recv_sem.at[piece, mask],
+            device_id={"dp": peers[lowest(mask)]},
+            device_id_type=MESH,
+        ).wait_recv()
+
+    for step in reversed(range(steps)):
         for piece in range(pieces):
-            turn = wave - piece
-            if turn >= 1 and turn <= steps:
-                copies[piece, turn - 1].wait_recv()
-            if turn >= 0 and turn < steps:
-                step = steps - 1 - turn
-                held = out_ref.at[piece, pl.ds(starts[step], count >> (step + 1))]
-                copies[piece, turn] = pltpu.make_async_remote_copy(
-                    src_ref=held,
-                    dst_ref=held,
-                    send_sem=send_sem.at[piece, turn],
-                    recv_sem=recv_sem.at[piece, turn],
-                    device_id={"dp": peers[step]},
-                    device_id_type=MESH,
-                )
-                copies[piece, turn].start()
-    for copy in copies.values():
+            send(piece, 0, step)
+    for mask in reversed(send_order(steps)):
+        for piece in range(pieces):
+            arrive(piece, mask)
+            for step in reversed(range(lowest(mask))):
+                send(piece, mask, step)
+    for piece in range(pieces):
+        for mask in range(1, 2**steps, 2):
+            arrive(piece, mask)
+    for copy in sends:
         copy.wait_send()
 
 
 def reduce_kernel(steps, pieces, x_ref, out_ref, work_ref, recv_ref, send_sem, recv_sem):
-    count = 2**steps
     bits, peers = partners(lax.axis_index("dp"), steps)
     greet(peers)
     copies = {}
 
-    def send(piece, step, source):
-        size = count >> (step + 1)
-        copies[piece, step] = pltpu.make_async_remote_copy(
+    def send(piece, mask, source):
+        copies[piece, mask] = pltpu.make_async_remote_copy(
             src_ref=source,
-            dst_ref=recv_ref.at[piece, pl.ds(size, size)],
-            send_sem=send_sem.at[piece, step],
-            recv_sem=recv_sem.at[piece, step],
-            device_id={"dp": peers[step]},
+            dst_ref=recv_ref.at[piece, mask],
+            send_sem=send_sem.at[piece, mask],
+            recv_sem=recv_sem.at[piece, mask],
+            device_id={"dp": peers[lowest(mask)]},
             device_id_type=MESH,
         )
-        copies[piece, step].start()
-
-    def total(piece, step, place):
-        size = count >> (step + 1)
-        if step == 0:
-            mine = x_ref[piece, bits[0] * size + place]
-        else:
-            mine = work_ref[piece, 2 * size + bits[step] * size + place]
-        theirs = recv_ref[piece, size + place]
-        return mine.astype(jnp.float32) + theirs.astype(jnp.float32)
-
-    def add_range(piece, step, first, length):
-        size = count >> (step + 1)
-
-        def body(index, carry):
-            place = first + index
-            work_ref[piece, size + place] = total(piece, step, place).astype(jnp.bfloat16)
-            return carry
-
-        lax.fori_loop(0, length, body, 0)
-
+        copies[piece, mask].start()
+
+    def total(piece, mask, count):
+        value = x_ref[piece, chunk_of(bits, mask)].astype(jnp.float32)
+        for step in range(count):
+            copies[piece, mask | 1 << step].wait_recv()
+            value = value + recv_ref[piece, mask | 1 << step].astype(jnp.float32)
+        return value
+
+    for mask in reversed(range(1, 2**steps, 2)):
+        for piece in range(pieces):
+            send(piece, mask, x_ref.at[piece, chunk_of(bits, mask)])
+    for mask in send_order(steps):
+        for piece in range(pieces):
+            work_ref[piece, mask] = total(piece, mask, lowest(mask)).astype(jnp.bfloat16)
+            send(piece, mask, work_ref.at[piece, mask])
     for piece in range(pieces):
-        half = count // 2
-        send(piece, 0, x_ref.at[piece, pl.ds((1 - bits[0]) * half, half)])
-    for wave in range(steps + pieces - 1):
-        for piece in range(pieces):
-            step = wave - piece
-            if step < 0 or step >= steps:
-                continue
-            copies[piece, step].wait_recv()
-            if step == steps - 1:
-                out_ref[piece] = total(piece, step, 0)
-                continue
-            size = count >> (step + 1)
-            part = size // 2
-            away = (1 - bits[step + 1]) * part
-            add_range(piece, step, away, part)
-            send(piece, step + 1, work_ref.at[piece, pl.ds(size + away, part)])
-            add_range(piece, step, bits[step + 1] * part, part)
+        out_ref[piece] = total(piece, 0, steps)
     for copy in copies.values():
         copy.wait_send()
-
-
-def bit_reversed(array, steps):
-    split = array.reshape((array.shape[0],) + (2,) * steps + array.shape[2:])
-    tail = tuple(range(steps + 1, split.ndim))
-    turned = split.transpose((0,) + tuple(range(steps, 0, -1)) + tail)
-    return turned.reshape(array.shape)
 
 
 def gather(packed, count):
     pieces, rows, lanes = packed.shape
     steps = count.bit_length() - 1
-    full = pl.pallas_call(
+    return pl.pallas_call(
         functools.partial(gather_kernel, steps, pieces),
         out_shape=jax.ShapeDtypeStruct((pieces, count, rows, lanes), packed.dtype),
         in_specs=[pl.BlockSpec(memory_space=pltpu.VMEM)],
         out_specs=pl.BlockSpec(memory_space=pltpu.VMEM),
-        scratch_shapes=[pltpu.SemaphoreType.DMA((pieces, steps))] * 2,
+        scratch_shapes=[pltpu.SemaphoreType.DMA((pieces, count))] * 2,
         compiler_params=pltpu.CompilerParams(
             collective_id=0, has_side_effects=True, vmem_limit_bytes=24 << 20
         ),
     )(packed)
-    return bit_reversed(full, steps)
 
 
 def reduce_scatter(packed, count):
@@ -195,13 +204,13 @@
         scratch_shapes=[
             pltpu.VMEM(packed.shape, jnp.bfloat16),
             pltpu.VMEM(packed.shape, jnp.bfloat16),
-            pltpu.SemaphoreType.DMA((pieces, steps)),
-            pltpu.SemaphoreType.DMA((pieces, steps)),
+            pltpu.SemaphoreType.DMA((pieces, count)),
+            pltpu.SemaphoreType.DMA((pieces, count)),
         ],
         compiler_params=pltpu.CompilerParams(
             collective_id=1, has_side_effects=True, vmem_limit_bytes=40 << 20
         ),
-    )(bit_reversed(packed, steps))
+    )(packed)
 
 
 def pack(blocks, gains):

time: 105 us -> 92.5 us (0.88)
  Pallas kernels: 63.6 us -> 52.2 us
    pallas_call x1, Pallas kernels: 32.6 us -> 26.5 us  [gather(): pl.pallas_call(functools.partial(gather_kernel, steps, pieces), out_shape...]
    pallas_call x1, Pallas kernels: 31.1 us -> 25.7 us  [reduce_scatter(): pl.pallas_call(functools.partial(reduce_kernel, steps, pieces), out_shape...]
    another operation x1 -> x4, other arithmetic: 0.86 us -> 2.29 us  [pack(): return jnp.stack(pieces)]
    concatenate x2 -> x0, other arithmetic: 1.13 us -> none  [pack(): jnp.concatenate([block[:, :, lane:lane + LANES], gain_rows], axis=1)]
where the time goes in v2:
time: 92.5 us; the launch traced here: 92.1 us
  Pallas kernels  52.2 us (56%)
  matrix products  23.2 us (25%)
  local copies, waits for them, and re-layouts  10.9 us (12%)
  other arithmetic  4.86 us (5%)
  between operations  0.94 us (1%)
    pallas_call x1, Pallas kernels, gather(): pl.pallas_call(functools.partial(gather_kernel, steps, pieces), out_shape...  26.5 us
    pallas_call x1, Pallas kernels, reduce_scatter(): pl.pallas_call(functools.partial(reduce_kernel, steps, pieces), out_shape...  25.7 us
    conv_general_dilated x4, matrix products, convolve(): lax.conv_general_dilated(inputs[None], kernel, (1, 1, 1), ((1, 1),) * 3,...  14.7 us
    conv_general_dilated x2, matrix products, weight_grad(): lax.conv_general_dilated(inputs[None], grad_out[None], (1, 1, 1), ((1, 1)...  8.52 us
    unnamed x22, local copies, waits for them, and re-layouts  3.44 us
    rev x2, local copies, waits for them, and re-layouts, transposed(): flipped = weight.reshape(27, channels, -1)[::-1]  2.33 us
    another operation x4, other arithmetic, pack(): return jnp.stack(pieces)  2.29 us

profile of v2, /device:TPU:0, one launch (start us, length us, event | category | flops | bytes accessed | tf_op | source)
XLA Modules:
  0.0 92.1 jit_solution(17923182664406624740)
XLA Ops:
  0.6 0.9 fusion.61
  1.5 0.9 fusion.47
  2.4 26.5 %shard_map.101 = bf16[3,16,224,128]{3,2,1,0:T(8,128)(2,1)S(1)} custom-call(bf16[3,224,128]{2,1,0:T(8,128)(2,1)S(1)} %maximum_bitcast_fusion.x_ref), custom_call_target="tpu_custom_call" | custom-call | tf_op jit(solution)/shard_map/pallas_call | solution.py:184
  29.0 1.5 %fusion.59 = (bf16[1,16,216,128]{3,2,1,0:T(8,128)(2,1)}, bf16[1,16,216,128]{3,2,1,0:T(8,128)(2,1)}, bf16[1,16,216,128]{3,2,1,0:T(8,128)(2,1)}) fusion(bf16[3,16,224,128]{3,2,1,0:T(8,128)(2,1)S(1)} %shard_map.101), kind=kLoop, calls=%fused_computation.104 | loop fusion | bytes 5308416 | tf_op jit(solution)/shard_map/slice | solution.py:243
  30.6 7.1 %fusion.62 = (f32[128]{0:T(128)S(1)}, f32[1,4,16,16,128]{4,0,3,2,1:T(1,128)S(1)}) fusion(bf16[3,3,3,128,128]{4,3,2,1,0:T(8,128)(2,1)} %bitcast.104, bf16[1,4,16,16,128]{4,3,2,1,0:T(8,128)(2,1)S(1)} %bitcast.116), kind=kOutput, calls=%fused_computation.107 | convolution fusion | flops 693501824 | bytes 1671680 | tf_op jit(solution)/shard_map/conv_general_dilated | solution.py:18
  38.2 1.3 %fusion.63 = (f32[256]{0:T(256)S(1)}, f32[1,2,8,8,256]{4,0,3,2,1:T(1,128)S(1)}) fusion(bf16[3,3,3,128,128]{4,3,2,1,0:T(8,128)(2,1)S(1)} %bitcast.102, bf16[3,3,3,128,128]{4,3,2,1,0:T(8,128)(2,1)S(1)} %bitcast.100, bf16[1,2,8,8,128]{4,3,2,1,0:T(8,128)(2,1)S(1)} %fusion.50), kind=kOutput, calls=%fused_computation.108 | convolution fusion | flops 130449152 | bytes 1934336 | tf_op jit(solution)/shard_map/conv_general_dilated | solution.py:18
  40.0 1.0 %rev.7 = bf16[27,128,128]{2,1,0:T(8,128)(2,1)} reverse(bf16[27,128,128]{2,1,0:T(8,128)(2,1)S(1)} %bitcast.105), dimensions={0} | reverse | bytes 1769472 | tf_op jit(solution)/shard_map/rev | solution.py:42
  41.0 1.1 %convolution_convert_fusion = bf16[3,3,3,128,256]{4,3,2,1,0:T(8,128)(2,1)S(1)} fusion(bf16[1,2,8,8,256]{4,3,2,1,0:T(8,128)(2,1)S(1)} %fusion.41, bf16[1,2,8,8,128]{4,3,2,1,0:T(8,128)(2,1)S(1)} %fusion.50), kind=kOutput, calls=%fused_computation.9 | convolution fusion | flops 127762432 | bytes 1867776 | tf_op jit(solution)/shard_map/conv_general_dilated | solution.py:29
  42.4 1.1 %fusion.15 = (bf16[1,16,224,128]{3,2,1,0:T(8,128)(2,1)S(1)}, bf16[1,16,224,128]{3,2,1,0:T(8,128)(2,1)}) fusion(bf16[16,1,16]{2,1,0:T(2,128)(2,1)S(1)} %convert_element_type.137, bf16[16,216,128]{2,1,0:T(8,128)(2,1)S(1)} %get-tuple-element.29, bf16[16,216,128]{2,1,0:T(8,128)(2,1)S(1)} %get-tuple-element.30), kind=kLoop, calls=%fused_computation.23 | loop fusion | flops 4128768 | bytes 3604992 | tf_op jit(solution)/shard_map/stack | solution.py:228
  43.8 0.4 copy-done.4
  44.4 1.3 %rev.6 = bf16[27,128,256]{2,1,0:T(8,128)(2,1)} reverse(bf16[27,128,256]{2,1,0:T(8,128)(2,1)S(1)} %pad_maximum_fusion.1), dimensions={0} | reverse | bytes 3538944 | tf_op jit(solution)/shard_map/rev | solution.py:42
  45.7 3.3 %fusion.9 = f32[1,2,8,8,128]{4,0,3,2,1:T(1,128)S(1)} fusion(bf16[3,3,3,256,128]{3,4,2,1,0:T(8,128)(2,1)} %bitcast.106, bf16[1,2,8,8,256]{4,3,2,1,0:T(8,128)(2,1)S(1)} %fusion.41), kind=kOutput, calls=%fused_computation.17 | convolution fusion | flops 126926848 | bytes 1900544 | tf_op jit(solution)/shard_map/conv_general_dilated | solution.py:18
  49.3 0.3 multiply_reduce_fusion
  49.6 0.3 fusion.58
  50.5 0.8 copy-done.6
  51.3 2.9 %fusion.7 = bf16[4,16,8,3,128]{4,2,3,1,0:T(8,128)(2,1)S(1)} fusion(bf16[3,3,3,128,128]{3,4,2,1,0:T(8,128)(2,1)S(1)} %bitcast.109, bf16[4,16,1,7,2,128]{5,3,4,1,0,2:T(8,128)(2,1)S(1)} %slice.60, bf16[4,16,1,8,3,128]{5,3,4,1,0,2:T(8,128)(2,1)S(1)} %copy.64, pred[8,3]{0,1:T(4,128)(4,1)S(1)} %copy-done.9), kind=kOutput, calls=%fused_computation.14 | convolution fusion | flops 1087635456 | bytes 1900568 | tf_op jit(solution)/shard_map/conv_general_dilated | solution.py:18
  54.3 0.8 copy.73
  55.1 7.4 %convolution_convert_fusion.1 = bf16[3,3,3,128,128]{4,3,2,1,0:T(8,128)(2,1)S(1)} fusion(bf16[1,4,16,16,128]{4,3,2,1,0:T(8,128)(2,1)S(1)} %add_convert_fusion, bf16[1,4,16,16,128]{4,3,2,1,0:T(8,128)(2,1)S(1)} %bitcast.117), kind=kOutput, calls=%fused_computation.10 | convolution fusion | flops 693813248 | bytes 1409024 | tf_op jit(solution)/shard_map/conv_general_dilated | solution.py:29
  62.6 1.1 %copy-done = bf16[1,16,224,128]{3,2,1,0:T(8,128)(2,1)S(1)} copy-done((bf16[1,16,224,128]{3,2,1,0:T(8,128)(2,1)S(1)}, bf16[1,16,224,128]{3,2,1,0:T(8,128)(2,1)}, u32[]{:S(2)}) %copy-start) | copy-done | bytes 917528
  64.0 25.7 %shard_map.102 = f32[3,224,128]{2,1,0:T(8,128)S(1)} custom-call(bf16[3,16,224,128]{3,2,1,0:T(8,128)(2,1)S(1)} %pad_maximum_fusion.x_ref), custom_call_target="tpu_custom_call" | custom-call | tf_op jit(solution)/shard_map/pallas_call | solution.py:199
  89.7 0.5 slice_bitcast_fusion.5
  90.2 0.5 slice_bitcast_fusion.4
  90.7 0.7 slice_bitcast_fusion.2
  91.4 0.7 pad_maximum_fusion.2
  (52 shorter events, 3.1 us)
Async XLA Ops:
  29.0 1.6 %copy-start.8 = (bf16[4,16,16,128]{3,2,1,0:T(8,128)(2,1)S(1)}, bf16[4,16,16,128]{3,2,1,0:T(8,128)(2,1)}, u32[]{:S(2)}) copy-start(bf16[4,16,16,128]{3,2,1,0:T(8,128)(2,1)} %param.6) | copy-start | bytes 786436
  30.6 7.5 %copy-start.1 = (bf16[1,16,216,128]{3,2,1,0:T(8,128)(2,1)S(1)}, bf16[1,16,216,128]{3,2,1,0:T(8,128)(2,1)}, u32[]{:S(2)}) copy-start(bf16[1,16,216,128]{3,2,1,0:T(8,128)(2,1)} %get-tuple-element.26) | copy-start | bytes 2654212
  30.6 7.5 %copy-start.3 = (bf16[1,16,216,128]{3,2,1,0:T(8,128)(2,1)S(1)}, bf16[1,16,216,128]{3,2,1,0:T(8,128)(2,1)}, u32[]{:S(2)}) copy-start(bf16[1,16,216,128]{3,2,1,0:T(8,128)(2,1)} %get-tuple-element.27) | copy-start | bytes 2654212
  38.1 1.4 %copy-start.7 = (bf16[2,8,8,256]{3,2,1,0:T(8,128)(2,1)S(1)}, bf16[2,8,8,256]{3,2,1,0:T(8,128)(2,1)}, u32[]{:S(2)}) copy-start(bf16[2,8,8,256]{3,2,1,0:T(8,128)(2,1)} %param.7) | copy-start | bytes 196612
  38.1 1.9 %copy-start.5 = (bf16[1,16,216,128]{3,2,1,0:T(8,128)(2,1)S(1)}, bf16[1,16,216,128]{3,2,1,0:T(8,128)(2,1)}, u32[]{:S(2)}) copy-start(bf16[1,16,216,128]{3,2,1,0:T(8,128)(2,1)} %get-tuple-element.28) | copy-start | bytes 2654212
  42.4 1.4 %copy-start.2 = (bf16[1,16,216,128]{3,2,1,0:T(8,128)(2,1)S(1)}, bf16[1,16,216,128]{3,2,1,0:T(8,128)(2,1)}, u32[]{:S(2)}) copy-start(bf16[1,16,216,128]{3,2,1,0:T(8,128)(2,1)} %get-tuple-element.26) | copy-start | bytes 2654212
  42.4 1.8 %copy-start.4 = (bf16[1,16,216,128]{3,2,1,0:T(8,128)(2,1)S(1)}, bf16[1,16,216,128]{3,2,1,0:T(8,128)(2,1)}, u32[]{:S(2)}) copy-start(bf16[1,16,216,128]{3,2,1,0:T(8,128)(2,1)} %get-tuple-element.27) | copy-start | bytes 2654212
  50.1 1.2 %copy-start.6 = (bf16[27,128,128]{2,1,0:T(8,128)(2,1)S(1)}, bf16[27,128,128]{2,1,0:T(8,128)(2,1)}, u32[]{:S(2)}) copy-start(bf16[27,128,128]{2,1,0:T(8,128)(2,1)} %rev.7) | copy-start | bytes 2654212
  50.1 1.2 %copy-start.9 = (pred[8,3]{0,1:T(4,128)(4,1)S(1)}, pred[8,3]{0,1:T(4,128)(4,1)}, u32[]{:S(2)}) copy-start(pred[8,3]{0,1:T(4,128)(4,1)} %constant.49) | copy-start | bytes 76
  62.5 1.2 %copy-start = (bf16[1,16,224,128]{3,2,1,0:T(8,128)(2,1)S(1)}, bf16[1,16,224,128]{3,2,1,0:T(8,128)(2,1)}, u32[]{:S(2)}) copy-start(bf16[1,16,224,128]{3,2,1,0:T(8,128)(2,1)} %get-tuple-element.37) | copy-start | bytes 2752516
